TPU v7x, 256 devices: a whole 4x4x8 slice. The times are simulated.
256 devices in a mesh: section: 32 (over y, z_lo, core), head: 8 (over x, z_hi).
Axes of the slice: x: 4, y: 4, z: 8 (z_hi: 2, z_lo: 4; z = z_hi * 4 + z_lo), core: 2. Of those that a mesh axis runs over, the one named last changes fastest.
Arguments:
- carry_x: bfloat16 [32, 384, 1152], P('section', 'head'), may hold values from -6 to 6
- kv_buffer: bfloat16 [32, 2, 1152, 6144], P('section', None, 'head'), may hold values from -48 to 48, as said below
- qkv_weight: bfloat16 [32, 3, 1152, 1152], P('section', None, 'head'), may hold values from -0.1875 to 0.1875
- out_weight: bfloat16 [32, 1152, 1152], P('section', 'head'), may hold values from -0.1875 to 0.1875
- up_weight: bfloat16 [32, 1152, 4608], P('section', None, 'head'), may hold values from -0.1875 to 0.1875
- down_weight: bfloat16 [32, 1152, 4608], P('section', None, 'head'), may hold values from -0.09375 to 0.09375
- time_table: float32 [20, 6, 1152], replicated, may hold values from -3 to 3
- block_table: float32 [32, 6, 1152], P('section'), may hold values from -3 to 3
- time_index: int32 [32], P('section'), may hold values from 0 to 19
- patch_order: int32 [16], replicated, may hold values from 0 to 15, each once
Outputs:
- next_x: bfloat16 [32, 384, 1152], P('section', 'head')
- fresh_kv: bfloat16 [32, 2, 2, 1152, 384], P('section', None, None, 'head')
Inputs may be any that keep to these rules, and one draw needn't show every extreme that they name: `kv_buffer`: cached keys and values.
All inputs are finite; a program needn't handle non-finite values.
Results may differ from a plain program's by a relative error of at most 0.034.
Values may be sent and summed in bfloat16 or wider, within the bound.
No kernel may reach another device: no remote copies, remote signals or barrier semaphores. Data moves between devices by JAX's collectives and lax.ppermute only.
A program may use at most 128 MiB of HBM per device.

v0:
```python
import math

import jax
import jax.numpy as jnp
from jax import lax
from jax.sharding import PartitionSpec as P

HEAD_DIM = 72
PATCHES = 16
MICRO = 2
STEPS = 20


def passed_along(value, axis, steps):
    count = lax.axis_size(axis)
    pairs = [(source, (source + steps) % count) for source in range(count)]
    return lax.ppermute(value, axis, pairs)


def layer_norm(values_in):
    center = values_in - jnp.mean(values_in, axis=-1, keepdims=True)
    spread = jnp.mean(center * center, axis=-1, keepdims=True)
    return center * lax.rsqrt(spread + 1e-06)


def patch_of(patch_order, section_index, micro):
    position = (micro - section_index) % PATCHES
    picked = jnp.where(jnp.arange(PATCHES) == position, patch_order, 0)
    return jnp.sum(picked)


def attend(queries, key_cache, value_cache, heads_dev):
    head_queries = queries.reshape(queries.shape[0], heads_dev, HEAD_DIM)
    head_keys = key_cache.reshape(heads_dev, HEAD_DIM, key_cache.shape[1])
    head_values = value_cache.reshape(heads_dev, HEAD_DIM, value_cache.shape[1])
    scores = jnp.einsum(
        "qhd,hdk->hqk", head_queries, head_keys, preferred_element_type=jnp.float32
    ) / math.sqrt(HEAD_DIM)
    probs = jax.nn.softmax(scores, axis=-1).astype(jnp.bfloat16)
    attended = jnp.einsum("hqk,hdk->qhd", probs, head_values, preferred_element_type=jnp.float32)
    return attended.astype(jnp.bfloat16).reshape(queries.shape[0], heads_dev * HEAD_DIM)


def local(
    carry_x,
    kv_buffer,
    qkv_weight,
    out_weight,
    up_weight,
    down_weight,
    time_table,
    block_table,
    time_index,
    patch_order,
):
    section_index = lax.axis_index("section")
    w_qkv = qkv_weight[0]
    w_out = out_weight[0]
    w_up = up_weight[0]
    w_down = down_weight[0]
    local_width = w_qkv.shape[1]
    heads_dev = local_width // HEAD_DIM
    chosen = jnp.arange(STEPS) == time_index[0]
    modulation = (
        jnp.sum(jnp.where(chosen[:, None, None], time_table, jnp.float32(0.0)), axis=0)
        + block_table[0]
    )
    inputs = carry_x[0]
    key_cache = kv_buffer[0, 0]
    value_cache = kv_buffer[0, 1]
    fresh_list = []
    for micro in range(MICRO):
        patch = patch_of(patch_order, section_index, micro)
        normed = (
            layer_norm(lax.all_gather(inputs, "head", axis=0, tiled=True).astype(jnp.float32))
            * (1.0 + modulation[1])
            + modulation[0]
        )
        projected = jnp.einsum(
            "td,ced->tce", normed.astype(jnp.bfloat16), w_qkv, preferred_element_type=jnp.float32
        ).astype(jnp.bfloat16)
        queries = projected[:, 0]
        new_keys = projected[:, 1].T
        new_values = projected[:, 2].T
        patch_start = patch * projected.shape[0]
        key_cache = lax.dynamic_update_slice(key_cache, new_keys, (0, patch_start))
        value_cache = lax.dynamic_update_slice(value_cache, new_values, (0, patch_start))
        attended = attend(queries, key_cache, value_cache, heads_dev)
        mixed = lax.psum_scatter(
            jnp.dot(attended, w_out, preferred_element_type=jnp.float32),
            "head",
            scatter_dimension=0,
            tiled=True,
        )
        after_attn = inputs.astype(jnp.float32) + modulation[2] * mixed
        mlp_in = (layer_norm(after_attn) * (1.0 + modulation[4]) + modulation[3]).astype(
            jnp.bfloat16
        )
        hidden = jax.nn.gelu(
            jnp.dot(
                lax.all_gather(mlp_in, "head", axis=0, tiled=True),
                w_up,
                preferred_element_type=jnp.float32,
            ),
            approximate=True,
        ).astype(jnp.bfloat16)
        feedforward = lax.psum_scatter(
            lax.dot_general(
                hidden, w_down, (((1,), (1,)), ((), ())), preferred_element_type=jnp.float32
            ),
            "head",
            scatter_dimension=0,
            tiled=True,
        )
        outgoing = (after_attn + modulation[5] * feedforward).astype(jnp.bfloat16)
        fresh_list.append(jnp.stack([new_keys, new_values]))
        inputs = passed_along(outgoing, "section", 1)
    return (inputs[None], jnp.stack(fresh_list)[None])


def solution(mesh):
    placed = (
        P("section", "head", None),
        P("section", None, "head", None),
        P("section", None, "head", None),
        P("section", "head", None),
        P("section", None, "head"),
        P("section", None, "head"),
        P(),
        P("section", None, None),
        P("section"),
        P(),
    )
    return jax.shard_map(
        local,
        mesh=mesh,
        in_specs=placed,
        out_specs=(P("section", "head", None), P("section", None, None, "head", None)),
        check_vma=False,
    )
```

profile of v0, /device:TPU:2, one launch (start us, length us, event | category | flops | bytes accessed | tf_op | source)
XLA Modules:
  0.0 723.8 jit_solution(14890922663128104329)
XLA Ops:
  8.0 1.3 fusion.92
  10.0 1.3 select_reduce_fusion
  11.3 0.8 bitcast_add_fusion
  12.1 0.6 slice_reduce_fusion.1
  12.7 58.2 %all-gather = bf16[1,384,1152]{2,1,0:T(8,128)(2,1)S(1)} all-gather(bf16[1,48,1152]{2,1,0:T(8,128)(2,1)} %param.10), channel_id=2, replica_groups=mesh['section'=32,'head'=8] {'head'}, dimensions={1}, use_global_device_ids=true | all-gather | bytes 995328 | tf_op jit(solution)/shard_map/all_gather | solution.py:75
  71.0 0.2 convert_reduce_fusion
  71.2 0.4 fusion.21
  71.6 0.9 convolution_convert_fusion.1
  72.5 0.7 slice_bitcast_fusion.4
  73.2 0.4 copy-done.1
  73.7 1.5 slice_bitcast_fusion
  75.2 0.7 bitcast_dynamic-update-slice_fusion.3
  75.9 8.7 %fusion.107 = f32[2,384,6144]{2,1,0:T(8,128)} fusion(bf16[384,2,72]{0,2,1:T(8,128)(2,1)} %bitcast.137, bf16[2,72,6144]{2,1,0:T(8,128)(2,1)S(1)} %bitcast.133), kind=kOutput, calls=%fused_computation.143 | convolution fusion | flops 679477248 | bytes 20754432 | tf_op jit(solution)/shard_map/qhd,hdk->hqk/dot_general | solution.py:36
  84.6 21.0 %fusion.105 = (f32[2,384]{1,0:T(2,128)S(1)}, f32[2,384,6144]{2,1,0:T(8,128)}) fusion(f32[2,384,6144]{2,1,0:T(8,128)} %fusion.107), kind=kOutput, calls=%fused_computation.141 | output fusion | flops 18880512 | bytes 37751808 | tf_op jit(solution)/shard_map/sub | solution.py:39
  105.6 10.0 %fusion.34 = bf16[2,72,384]{2,1,0:T(8,128)(2,1)S(1)} fusion(bf16[2,72,6144]{2,1,0:T(8,128)(2,1)} %bitcast.135, f32[2,384,6144]{2,1,0:T(8,128)} %get-tuple-element.23, f32[2,384]{1,0:T(2,128)S(1)} %get-tuple-element.22), kind=kOutput, calls=%fused_computation.46 | convolution fusion | flops 688969728 | bytes 20757504 | tf_op jit(solution)/shard_map/hqk,hdk->qhd/dot_general | solution.py:40
  115.6 1.7 fusion.87
  117.3 94.5 %reduce-scatter.5.cloned.1.call-done = f32[48,1152]{1,0:T(8,128)} async-done(((f32[384,1152]{1,0:T(8,128)}), f32[48,1152]{1,0:T(8,128)}) %reduce-scatter.5.cloned.1.call-update) | async-done | bytes 221200 | tf_op jit(solution)/shard_map/reduce_scatter | solution.py:89
  211.9 1.1 fusion.104
  213.0 1.1 multiply_reduce_fusion.3
  214.1 1.1 add_convert_fusion.3
  215.2 52.7 %all_gather.13 = bf16[384,1152]{1,0:T(8,128)(2,1)} all-gather(bf16[48,1152]{1,0:T(8,128)(2,1)S(1)} %add_convert_fusion.3), channel_id=1, replica_groups=mesh['section'=32,'head'=8] {'head'}, dimensions={0}, use_global_device_ids=true | all-gather | bytes 995328 | tf_op jit(solution)/shard_map/all_gather | solution.py:101
  267.9 4.9 fusion.27
  272.8 91.6 %reduce-scatter.7.cloned.1.call-done = f32[48,1152]{1,0:T(8,128)} async-done(((f32[384,1152]{1,0:T(8,128)}), f32[48,1152]{1,0:T(8,128)}) %reduce-scatter.7.cloned.1.call-update) | async-done | bytes 221200 | tf_op jit(solution)/shard_map/reduce_scatter | solution.py:107
  364.4 1.6 add_convert_fusion.2
  366.6 7.7 %collective-permute-done = bf16[48,1152]{1,0:T(8,128)(2,1)S(1)} collective-permute-done((bf16[48,1152]{1,0:T(8,128)(2,1)}, bf16[48,1152]{1,0:T(8,128)(2,1)S(1)}, u32[]{:S(2)}, u32[]{:S(2)}) %collective-permute-start) | collective-permute-done | bytes 110624 | tf_op jit(solution)/shard_map/ppermute | solution.py:17
  374.3 47.7 %all_gather.14 = bf16[384,1152]{1,0:T(8,128)(2,1)S(1)} all-gather(bf16[48,1152]{1,0:T(8,128)(2,1)S(1)} %collective-permute-done), channel_id=1, replica_groups=mesh['section'=32,'head'=8] {'head'}, dimensions={0}, use_global_device_ids=true | all-gather | bytes 995328 | tf_op jit(solution)/shard_map/all_gather | solution.py:75
  422.0 0.2 convert_reduce_fusion.1
  422.2 0.4 fusion.14
  422.7 0.9 convolution_convert_fusion
  423.6 0.7 slice_bitcast_fusion.2
  424.3 0.7 bitcast_dynamic-update-slice_fusion.1
  424.9 7.9 %fusion.108 = f32[2,384,6144]{2,1,0:T(8,128)} fusion(bf16[384,2,72]{0,2,1:T(8,128)(2,1)S(1)} %bitcast.138, bf16[2,72,6144]{2,1,0:T(8,128)(2,1)S(1)} %bitcast.134), kind=kOutput, calls=%fused_computation.144 | convolution fusion | flops 679477248 | bytes 20754432 | tf_op jit(solution)/shard_map/qhd,hdk->hqk/dot_general | solution.py:36
  432.8 21.5 %fusion.106 = (f32[2,384]{1,0:T(2,128)}, f32[2,384,6144]{2,1,0:T(8,128)}) fusion(f32[2,384,6144]{2,1,0:T(8,128)} %fusion.108), kind=kOutput, calls=%fused_computation.142 | output fusion | flops 18880512 | bytes 37751808 | tf_op jit(solution)/shard_map/sub | solution.py:39
  454.3 9.4 %fusion.33 = bf16[2,72,384]{2,1,0:T(8,128)(2,1)S(1)} fusion(bf16[2,72,6144]{2,1,0:T(8,128)(2,1)S(1)} %bitcast.136, f32[2,384,6144]{2,1,0:T(8,128)} %get-tuple-element.25, f32[2,384]{1,0:T(2,128)} %get-tuple-element.24), kind=kOutput, calls=%fused_computation.45 | convolution fusion | flops 688969728 | bytes 20757504 | tf_op jit(solution)/shard_map/hqk,hdk->qhd/dot_general | solution.py:40
  463.8 1.7 fusion.85
  465.6 91.9 %reduce-scatter.9.cloned.1.call-done = f32[48,1152]{1,0:T(8,128)} async-done(((f32[384,1152]{1,0:T(8,128)}), f32[48,1152]{1,0:T(8,128)}) %reduce-scatter.9.cloned.1.call-update) | async-done | bytes 221200 | tf_op jit(solution)/shard_map/reduce_scatter | solution.py:89
  557.5 1.1 fusion.103
  558.6 1.1 multiply_reduce_fusion.2
  559.7 1.0 add_convert_fusion.1
  560.8 51.1 %all_gather.15 = bf16[384,1152]{1,0:T(8,128)(2,1)S(1)} all-gather(bf16[48,1152]{1,0:T(8,128)(2,1)S(1)} %add_convert_fusion.1), channel_id=1, replica_groups=mesh['section'=32,'head'=8] {'head'}, dimensions={0}, use_global_device_ids=true | all-gather | bytes 995328 | tf_op jit(solution)/shard_map/all_gather | solution.py:101
  611.9 4.6 fusion.25
  616.5 0.9 copy-done.8
  617.4 90.0 %reduce-scatter.11.cloned.1.call-done = f32[48,1152]{1,0:T(8,128)} async-done(((f32[384,1152]{1,0:T(8,128)}), f32[48,1152]{1,0:T(8,128)}) %reduce-scatter.11.cloned.1.call-update) | async-done | bytes 221200 | tf_op jit(solution)/shard_map/reduce_scatter | solution.py:107
  707.4 1.0 add_convert_fusion
  708.4 0.1 collective-permute-start.1
  708.5 0.8 maximum_bitcast_fusion
  709.3 7.3 %collective-permute-done.1 = bf16[48,1152]{1,0:T(8,128)(2,1)S(1)} collective-permute-done((bf16[48,1152]{1,0:T(8,128)(2,1)S(1)}, bf16[48,1152]{1,0:T(8,128)(2,1)S(1)}, u32[]{:S(2)}, u32[]{:S(2)}) %collective-permute-start.1) | collective-permute-done | bytes 110624 | tf_op jit(solution)/shard_map/ppermute | solution.py:17
  716.6 0.6 copy.20
  (58 shorter events, 0.5 us)
Async XLA Ops:
  7.2 260.7 %copy-start = (bf16[1,1152,576]{1,2,0:T(8,128)(2,1)S(1)}, bf16[1,1152,576]{1,2,0:T(8,128)(2,1)}, u32[]{:S(2)}) copy-start(bf16[1,1152,576]{1,2,0:T(8,128)(2,1)} %param.15) | copy-start | bytes 3981316
  7.2 204.7 %reduce-scatter.5.cloned.1.call-start = ((), (), s32[]{:S(2)}) async-start(), calls=%async_computation.4 | async-start | bytes 1990656 | tf_op jit(solution)/shard_map/reduce_scatter | solution.py:89
  10.0 61.6 %copy-start.18 = (bf16[1,3,144,1152]{3,2,1,0:T(8,128)(2,1)S(1)}, bf16[1,3,144,1152]{3,2,1,0:T(8,128)(2,1)}, u32[]{:S(2)}) copy-start(bf16[1,3,144,1152]{3,2,1,0:T(8,128)(2,1)} %param.12) | copy-start | bytes 2985988
  12.7 58.8 %copy-start.14 = (f32[1152]{0:T(1024)}, f32[1152]{0:T(1024)S(1)}, u32[]{:S(2)}) copy-start(f32[1152]{0:T(1024)S(1)} %get-tuple-element.5) | copy-start | bytes 13828
  12.7 58.9 %copy-start.16 = (f32[1152]{0:T(1024)}, f32[1152]{0:T(1024)S(1)}, u32[]{:S(2)}) copy-start(f32[1152]{0:T(1024)S(1)} %get-tuple-element.6) | copy-start | bytes 13828
  71.6 2.1 copy-start.1
  105.6 10.0 %copy-start.6 = (bf16[1,144,1152]{2,1,0:T(8,128)(2,1)S(1)}, bf16[1,144,1152]{2,1,0:T(8,128)(2,1)}, u32[]{:S(2)}) copy-start(bf16[1,144,1152]{2,1,0:T(8,128)(2,1)} %param.13) | copy-start | bytes 995332
  115.6 96.3 %copy-start.4 = (bf16[1,48,1152]{2,1,0:T(8,128)(2,1)S(1)}, bf16[1,48,1152]{2,1,0:T(8,128)(2,1)}, u32[]{:S(2)}) copy-start(bf16[1,48,1152]{2,1,0:T(8,128)(2,1)} %param.10) | copy-start | bytes 331780
  117.3 96.9 %copy-start.10 = (f32[1152]{0:T(1024)S(1)}, f32[1152]{0:T(1024)}, u32[]{:S(2)}) copy-start(f32[1152]{0:T(1024)} %get-tuple-element.3) | copy-start | bytes 13828
  117.3 96.9 %copy-start.12 = (f32[1152]{0:T(1024)S(1)}, f32[1152]{0:T(1024)}, u32[]{:S(2)}) copy-start(f32[1152]{0:T(1024)} %get-tuple-element.4) | copy-start | bytes 13828
  117.3 247.1 %reduce-scatter.7.cloned.1.call-start = ((), (), s32[]{:S(2)}) async-start(), calls=%async_computation.5 | async-start | bytes 1990656 | tf_op jit(solution)/shard_map/reduce_scatter | solution.py:107
  272.7 91.6 %copy-start.3 = (f32[48,1152]{1,0:T(8,128)S(1)}, f32[48,1152]{1,0:T(8,128)}, u32[]{:S(2)}) copy-start(f32[48,1152]{1,0:T(8,128)} %reduce-scatter.5.cloned.1.call-done) | copy-start | bytes 663556
  272.8 284.7 %reduce-scatter.9.cloned.1.call-start = ((), (), s32[]{:S(2)}) async-start(), calls=%async_computation.6 | async-start | bytes 1990656 | tf_op jit(solution)/shard_map/reduce_scatter | solution.py:89
  366.0 56.6 %copy-start.15 = (f32[1152]{0:T(1024)S(1)}, f32[1152]{0:T(1024)}, u32[]{:S(2)}) copy-start(f32[1152]{0:T(1024)} %copy-done.14) | copy-start | bytes 13828
  366.0 56.6 %copy-start.17 = (f32[1152]{0:T(1024)S(1)}, f32[1152]{0:T(1024)}, u32[]{:S(2)}) copy-start(f32[1152]{0:T(1024)} %copy-done.16) | copy-start | bytes 13828
  366.0 8.3 %collective-permute-start = (bf16[48,1152]{1,0:T(8,128)(2,1)}, bf16[48,1152]{1,0:T(8,128)(2,1)S(1)}, u32[]{:S(2)}, u32[]{:S(2)}) collective-permute-start(bf16[48,1152]{1,0:T(8,128)(2,1)} %add_convert_fusion.2), channel_id=1, source_target_pairs={{0,8},{8,16},{16,24},{24,32},{32,40},{40,48},{48,56},{56,64},{64,7... | collective-permute-start | bytes 331784 | tf_op jit(solution)/shard_map/ppermute | solution.py:17
  366.6 56.0 %copy-start.19 = (bf16[1,3,144,1152]{3,2,1,0:T(8,128)(2,1)S(1)}, bf16[1,3,144,1152]{3,2,1,0:T(8,128)(2,1)}, u32[]{:S(2)}) copy-start(bf16[1,3,144,1152]{3,2,1,0:T(8,128)(2,1)} %param.12) | copy-start | bytes 2985988
  432.8 21.5 %copy-start.5 = (bf16[144,6144]{1,0:T(8,128)(2,1)S(1)}, bf16[144,6144]{1,0:T(8,128)(2,1)}, u32[]{:S(2)}) copy-start(bf16[144,6144]{1,0:T(8,128)(2,1)} %get-tuple-element.19) | copy-start | bytes 5308420
  454.3 9.4 %copy-start.7 = (bf16[1,144,1152]{2,1,0:T(8,128)(2,1)S(1)}, bf16[1,144,1152]{2,1,0:T(8,128)(2,1)}, u32[]{:S(2)}) copy-start(bf16[1,144,1152]{2,1,0:T(8,128)(2,1)} %param.13) | copy-start | bytes 995332
  465.5 94.2 %copy-start.11 = (f32[1152]{0:T(1024)S(1)}, f32[1152]{0:T(1024)}, u32[]{:S(2)}) copy-start(f32[1152]{0:T(1024)} %get-tuple-element.3) | copy-start | bytes 13828
  465.5 94.3 %copy-start.13 = (f32[1152]{0:T(1024)S(1)}, f32[1152]{0:T(1024)}, u32[]{:S(2)}) copy-start(f32[1152]{0:T(1024)} %get-tuple-element.4) | copy-start | bytes 13828
  465.5 241.9 %reduce-scatter.11.cloned.1.call-start = ((), (), s32[]{:S(2)}) async-start(), calls=%async_computation.7 | async-start | bytes 1990656 | tf_op jit(solution)/shard_map/reduce_scatter | solution.py:107
  616.5 0.9 copy-start.8
  616.5 0.9 copy-start.9
  616.5 91.0 %copy-start.2 = (f32[48,1152]{1,0:T(8,128)S(1)}, f32[48,1152]{1,0:T(8,128)}, u32[]{:S(2)}) copy-start(f32[48,1152]{1,0:T(8,128)} %reduce-scatter.9.cloned.1.call-done) | copy-start | bytes 663556
  708.4 8.2 %collective-permute-start.1 = (bf16[48,1152]{1,0:T(8,128)(2,1)S(1)}, bf16[48,1152]{1,0:T(8,128)(2,1)S(1)}, u32[]{:S(2)}, u32[]{:S(2)}) collective-permute-start(bf16[48,1152]{1,0:T(8,128)(2,1)S(1)} %add_convert_fusion), channel_id=1, source_target_pairs={{0,8},{8,16},{16,24},{24,32},{32,40},{40,48},{48,56},{56,64},{64,7... | collective-permute-start | bytes 331784 | tf_op jit(solution)/shard_map/ppermute | solution.py:17
Sparse Core Ops, SparseCore 0:
  117.4 94.4 reduce-scatter.4
  272.9 91.4 reduce-scatter.6
  465.6 91.8 reduce-scatter.8
  616.6 90.7 reduce-scatter.10
where the time goes:
time: 724 us
  waiting for transfers between devices  383 us (53%)
  blocking collectives  210 us (29%)
  other arithmetic  57.7 us (8%)
  matrix products  50.7 us (7%)
  between operations  16 us (2%)
    reduce_scatter x2, waiting for transfers between devices, local(): lax.psum_scatter(jnp.dot(attended, w_out, preferred_element_type=jnp.floa...  186 us
    reduce_scatter x2, waiting for transfers between devices, local(): lax.psum_scatter(lax.dot_general(hidden, w_down, (((1,), (1,)), ((), ()))...  182 us
    all_gather x2, blocking collectives, local(): lax.all_gather(inputs, 'head', axis=0, tiled=True).astype(jnp.float32)  106 us
    all_gather x2, blocking collectives, local(): lax.all_gather(mlp_in, 'head', axis=0, tiled=True)  104 us
    sub x2, other arithmetic, attend(): probs = jax.nn.softmax(scores, axis=-1).astype(jnp.bfloat16)  42.5 us
    dot_general x2, matrix products, attend(): jnp.einsum('hqk,hdk->qhd', probs, head_values, preferred_element_type=jnp...  19.4 us
    dot_general x2, matrix products, attend(): jnp.einsum('qhd,hdk->hqk', head_queries, head_keys, preferred_element_typ...  16.6 us
    ppermute x2, waiting for transfers between devices, passed_along(): return lax.ppermute(value, axis, pairs)  14.9 us
  transfers between devices with their start and end apart: 6, of which 6 were waited for; matrix products, arithmetic and copies ran while one was open for 0% of the time, Pallas kernels for 0%

commit v1 on v0

v1 whole, which is shorter than its diff:
```python
import functools
import math

import jax
import jax.numpy as jnp
from jax import lax
from jax.experimental import pallas as pl
from jax.experimental.pallas import tpu as pltpu
from jax.sharding import PartitionSpec as P

HEAD_DIM = 72
PATCHES = 16
PATCH_TOK = 384
MICRO = 2
STEPS = 20
COLUMNS = 4
SECTIONS = 32
PAIR = PATCH_TOK // COLUMNS
HALF = PAIR // 2
LOG2_SCALE = math.log2(math.e) / math.sqrt(HEAD_DIM)
NT = (((1,), (1,)), ((), ()))
F32 = jnp.float32
BF16 = jnp.bfloat16
VMEM = pl.BlockSpec(memory_space=pltpu.VMEM)
SMEM = pl.BlockSpec(memory_space=pltpu.SMEM)
ANY = pl.BlockSpec(memory_space=pl.ANY)


def head_of(column, row):
    return (column % COLUMNS) * 2 + row % 2


def flat(section, head):
    return (section % SECTIONS) * 8 + head


ROW_SWAP = [(head_of(c, r), head_of(c, r + 1)) for c in range(COLUMNS) for r in range(2)]


def column_step(step):
    return [(head_of(c, r), head_of(c + step, r)) for c in range(COLUMNS) for r in range(2)]


def section_step(step):
    return [
        (flat(s, head_of(c, r)), flat(s + 1, head_of(c + step, r + (s % 8 == 7))))
        for s in range(SECTIONS)
        for c in range(COLUMNS)
        for r in range(2)
    ]


def swap_rows(value):
    return lax.ppermute(value, "head", ROW_SWAP)


def to_column(value, step):
    return lax.ppermute(value, "head", column_step(step))


def to_section(value, step):
    return lax.ppermute(value, ("section", "head"), section_step(step))


def layer_norm(values_in):
    center = values_in - jnp.mean(values_in, axis=-1, keepdims=True)
    spread = jnp.mean(center * center, axis=-1, keepdims=True)
    return center * lax.rsqrt(spread + 1e-06)


def patch_of(patch_order, section_index, micro):
    position = (micro - section_index) % PATCHES
    picked = jnp.where(jnp.arange(PATCHES) == position, patch_order, 0)
    return jnp.sum(picked)


def attention_kernel(micro, patch_ref, x0, x1, x2, x3, mod, w_qkv, w_out, cache, *rest):
    if micro:
        earlier, rest = rest[0], rest[1:]
    fresh, part0, part1, part2, part3, keys, values, attn_in, queries, scores, sem = rest
    width = w_qkv.shape[1]
    copies = [
        pltpu.make_async_copy(
            cache.at[0, :, pl.ds(c * PATCH_TOK, PATCH_TOK)], keys.at[c], sem.at[0]
        )
        for c in range(PATCHES)
    ] + [
        pltpu.make_async_copy(
            cache.at[1, :, pl.ds(c * PATCH_TOK, PATCH_TOK)],
            values.at[c, pl.ds(0, width)],
            sem.at[1],
        )
        for c in range(PATCHES)
    ]
    for copy in copies:
        copy.start()
    for k, block in enumerate((x0, x1, x2, x3)):
        attn_in[k * PAIR : (k + 1) * PAIR, :] = (
            layer_norm(block[...].astype(F32)) * (1.0 + mod[1:2, :]) + mod[0:1, :]
        ).astype(BF16)
    normed = attn_in[...]
    projected = lax.dot_general(normed, w_qkv[0], NT, preferred_element_type=F32)
    first_head = lax.broadcasted_iota(jnp.int32, (PATCH_TOK, width), 1) < HEAD_DIM
    queries[0:PATCH_TOK, :] = jnp.where(first_head, projected, 0.0).astype(BF16)
    queries[PATCH_TOK : 2 * PATCH_TOK, :] = jnp.where(first_head, 0.0, projected).astype(BF16)
    new_keys = lax.dot_general(w_qkv[1], normed, NT, preferred_element_type=F32).astype(BF16)
    new_values = lax.dot_general(w_qkv[2], normed, NT, preferred_element_type=F32).astype(BF16)
    fresh[0] = new_keys
    fresh[1] = new_values
    values[:, width : width + 16, :] = jnp.ones((PATCHES, 16, PATCH_TOK), BF16)
    for copy in copies:
        copy.wait()
    if micro:
        keys[patch_ref[0]] = earlier[0]
        values[patch_ref[0], 0:width] = earlier[1]
    keys[patch_ref[micro]] = new_keys
    values[patch_ref[micro], 0:width] = new_values
    highest = None
    for c in range(PATCHES):
        block = jnp.dot(queries[...], keys[c], preferred_element_type=F32)
        scores[c] = block
        top = jnp.maximum(jnp.maximum(block[:, 0:128], block[:, 128:256]), block[:, 256:384])
        highest = top if highest is None else jnp.maximum(highest, top)
    offset = jnp.max(highest, axis=1, keepdims=True) * LOG2_SCALE
    total = None
    for c in range(PATCHES):
        probs = jnp.exp2(scores[c] * LOG2_SCALE - offset).astype(BF16)
        product = lax.dot_general(probs, values[c], NT, preferred_element_type=F32)
        total = product if total is None else total + product
    total = total[:, 0:width] / total[:, width : width + 1]
    attended = jnp.where(first_head, total[0:PATCH_TOK], total[PATCH_TOK : 2 * PATCH_TOK])
    mixed = jnp.dot(attended.astype(BF16), w_out[...], preferred_element_type=F32)
    for k, part in enumerate((part0, part1, part2, part3)):
        part[...] = mixed[k * PAIR : (k + 1) * PAIR].astype(BF16)


def attention(micro, patches, blocks, modulation, w_qkv, w_out, cache, earlier):
    width, model = w_qkv.shape[1], w_qkv.shape[2]
    extra = [earlier] if micro else []
    return pl.pallas_call(
        functools.partial(attention_kernel, micro),
        out_shape=[jax.ShapeDtypeStruct((2, width, PATCH_TOK), BF16)]
        + [jax.ShapeDtypeStruct((PAIR, model), BF16)] * COLUMNS,
        in_specs=[SMEM] + [VMEM] * 7 + [ANY] + [VMEM] * len(extra),
        out_specs=[VMEM] * 5,
        scratch_shapes=[
            pltpu.VMEM((PATCHES, width, PATCH_TOK), BF16),
            pltpu.VMEM((PATCHES, width + 16, PATCH_TOK), BF16),
            pltpu.VMEM((PATCH_TOK, model), BF16),
            pltpu.VMEM((2 * PATCH_TOK, width), BF16),
            pltpu.VMEM((PATCHES, 2 * PATCH_TOK, PATCH_TOK), F32),
            pltpu.SemaphoreType.DMA((2,)),
        ],
        compiler_params=pltpu.CompilerParams(vmem_limit_bytes=52 * 2**20),
        cost_estimate=pl.CostEstimate(
            flops=4 * 10**9, bytes_accessed=8 * 10**6, transcendentals=5 * 10**6
        ),
        name="attention",
    )(patches, *blocks, modulation, w_qkv, w_out, cache, *extra)


def mlp_in_kernel(x_ref, own, other, mod, after_ref, mlp_ref):
    mixed = own[...].astype(F32) + other[...].astype(F32)
    after = x_ref[...].astype(F32) + mod[2:3, :] * mixed
    after_ref[...] = after
    mlp_ref[...] = (layer_norm(after) * (1.0 + mod[4:5, :]) + mod[3:4, :]).astype(BF16)


def mlp_input(pair, own, other, modulation):
    return pl.pallas_call(
        mlp_in_kernel,
        out_shape=[
            jax.ShapeDtypeStruct(pair.shape, F32),
            jax.ShapeDtypeStruct(pair.shape, BF16),
        ],
        in_specs=[VMEM] * 4,
        out_specs=[VMEM] * 2,
        name="mlp_input",
    )(pair, own, other, modulation)


def mlp_kernel(x0, x1, x2, x3, w_up, w_down, mod, part0, part1, part2, part3, gathered):
    for k, block in enumerate((x0, x1, x2, x3)):
        gathered[k * PAIR : (k + 1) * PAIR, :] = block[...]
    lifted = jnp.dot(gathered[...], w_up[...], preferred_element_type=F32)
    hidden = jax.nn.gelu(lifted, approximate=True).astype(BF16)
    lowered = lax.dot_general(hidden, w_down[...], NT, preferred_element_type=F32) * mod[5:6, :]
    for k, part in enumerate((part0, part1, part2, part3)):
        part[...] = lowered[k * PAIR : (k + 1) * PAIR].astype(BF16)


def mlp(blocks, w_up, w_down, modulation):
    shape = blocks[0].shape
    return pl.pallas_call(
        mlp_kernel,
        out_shape=[jax.ShapeDtypeStruct(shape, BF16)] * COLUMNS,
        in_specs=[VMEM] * 7,
        out_specs=[VMEM] * COLUMNS,
        scratch_shapes=[pltpu.VMEM((PATCH_TOK, shape[1]), BF16)],
        compiler_params=pltpu.CompilerParams(vmem_limit_bytes=40 * 2**20),
        cost_estimate=pl.CostEstimate(
            flops=10**9, bytes_accessed=5 * 10**6, transcendentals=2 * 10**5
        ),
        name="mlp",
    )(*blocks, w_up, w_down, modulation)


def summed(blocks):
    return sum(block.astype(F32) for block in blocks)


def gather_columns(pair):
    return [pair] + [to_column(pair, -k) for k in range(1, COLUMNS)]


def local(
    carry_x,
    kv_buffer,
    qkv_weight,
    out_weight,
    up_weight,
    down_weight,
    time_table,
    block_table,
    time_index,
    patch_order,
):
    section_index = lax.axis_index("section")
    head_index = lax.axis_index("head")
    column = head_index // 2
    row = head_index % 2
    chosen = jnp.arange(STEPS) == time_index[0]
    modulation = (
        jnp.sum(jnp.where(chosen[:, None, None], time_table, jnp.float32(0.0)), axis=0)
        + block_table[0]
    )
    patches = jnp.stack([patch_of(patch_order, section_index, m) for m in range(MICRO)]).astype(
        jnp.int32
    )
    own = carry_x[0]
    partner = swap_rows(own)
    pair = jnp.where(
        row == 0, jnp.concatenate([own, partner]), jnp.concatenate([partner, own])
    )
    fresh_list = []
    for micro in range(MICRO):
        fresh, *parts = attention(
            micro,
            patches,
            gather_columns(pair),
            modulation,
            qkv_weight[0],
            out_weight[0],
            kv_buffer[0],
            fresh_list[0] if micro else None,
        )
        fresh_list.append(fresh)
        row_sum = summed(
            [parts[0]] + [to_column(parts[k], k) for k in range(1, COLUMNS)]
        ).astype(BF16)
        after_attn, mlp_in = mlp_input(pair, row_sum, swap_rows(row_sum), modulation)
        parts = mlp(gather_columns(mlp_in), up_weight[0], down_weight[0], modulation)
        residual = to_section(after_attn, 0)
        row_sum = summed([to_section(parts[k], k) for k in range(COLUMNS)])
        if micro + 1 < MICRO:
            row_sum = row_sum.astype(BF16)
            both = row_sum.astype(F32) + swap_rows(row_sum).astype(F32)
            pair = (residual + both).astype(BF16)
        else:
            mine = jnp.where(row == 0, row_sum[:HALF], row_sum[HALF:])
            theirs = jnp.where(row == 0, row_sum[HALF:], row_sum[:HALF]).astype(BF16)
            kept = jnp.where(row == 0, residual[:HALF], residual[HALF:])
            outgoing = (kept + (mine + swap_rows(theirs).astype(F32))).astype(BF16)
    rotated = jnp.stack(fresh_list)
    rotated = jnp.concatenate([rotated, rotated], axis=-1)
    begin = ((COLUMNS - column) % COLUMNS) * PAIR
    fresh_kv = lax.dynamic_slice_in_dim(rotated, begin, PATCH_TOK, axis=-1)
    return (outgoing[None], fresh_kv[None])


def solution(mesh):
    placed = (
        P("section", "head", None),
        P("section", None, "head", None),
        P("section", None, "head", None),
        P("section", "head", None),
        P("section", None, "head"),
        P("section", None, "head"),
        P(),
        P("section", None, None),
        P("section"),
        P(),
    )
    return jax.shard_map(
        local,
        mesh=mesh,
        in_specs=placed,
        out_specs=(P("section", "head", None), P("section", None, None, "head", None)),
        check_vma=False,
    )
```

time: 724 us -> 237 us (0.33)
  waiting for transfers between devices: 383 us -> 91.7 us
  blocking collectives: 210 us -> 0 us
  starting transfers between devices: 0.25 us -> 75.6 us
  matrix products: 50.7 us -> 0 us
  Pallas kernels: 0 us -> 49.7 us
  other arithmetic: 57.7 us -> 8.22 us
  between operations: 16 us -> 1.81 us
    reduce_scatter x4 -> x0, waiting for transfers between devices: 368 us -> none  [the longest x2 186 us: local(): lax.psum_scatter(jnp.dot(attended, w_out, preferred_element_type=jnp.floa...]
    all_gather x4 -> x0, blocking collectives: 210 us -> none  [the longest x2 106 us: local(): lax.all_gather(inputs, 'head', axis=0, tiled=True).astype(jnp.float32)]
    ppermute x2 -> x33, waiting for transfers between devices: 14.9 us -> 91.7 us  [the longest x18 37.4 us: to_column(): return lax.ppermute(value, 'head', column_step(step))]
    ppermute x2 -> x33, starting transfers between devices: 0.09 us -> 75.6 us  [the longest x18 35.2 us: to_column(): return lax.ppermute(value, 'head', column_step(step))]
    dot_general x10 -> x0, matrix products: 50.7 us -> none  [the longest x2 19.4 us: attend(): jnp.einsum('hqk,hdk->qhd', probs, head_values, preferred_element_type=jnp...]
    pallas_call x0 -> x6, Pallas kernels: none -> 49.7 us  [the longest x2 39.8 us: attention(): pl.pallas_call(functools.partial(attention_kernel, micro), out_shape=[jax...]
    sub x2 -> x0, other arithmetic: 42.5 us -> none  [attend(): probs = jax.nn.softmax(scores, axis=-1).astype(jnp.bfloat16)]
  transfers between devices with their start and end apart: 6 -> 33, of which waited for: 6 -> 30; matrix products, arithmetic and copies ran while one was open for 0% -> 4% of each run, Pallas kernels for 0% -> 0%
where the time goes in v1:
time: 237 us; the launch traced here: 233 us
  waiting for transfers between devices  91.7 us (39%)
  starting transfers between devices  75.6 us (32%)
  Pallas kernels  49.7 us (21%)
  other arithmetic  8.22 us (3%)
  local copies, waits for them, and re-layouts  5.61 us (2%)
    pallas_call x2, Pallas kernels, attention(): pl.pallas_call(functools.partial(attention_kernel, micro), out_shape=[jax...  39.8 us
    ppermute x18, waiting for transfers between devices, to_column(): return lax.ppermute(value, 'head', column_step(step))  37.4 us
    ppermute x18, starting transfers between devices, to_column(): return lax.ppermute(value, 'head', column_step(step))  35.2 us
    ppermute x5, waiting for transfers between devices, swap_rows(): return lax.ppermute(value, 'head', ROW_SWAP)  33.9 us
    ppermute x10, starting transfers between devices, to_section(): return lax.ppermute(value, ('section', 'head'), section_step(step))  23.4 us
    ppermute x10, waiting for transfers between devices, to_section(): return lax.ppermute(value, ('section', 'head'), section_step(step))  20.4 us
    ppermute x5, starting transfers between devices, swap_rows(): return lax.ppermute(value, 'head', ROW_SWAP)  17 us
    pallas_call x2, Pallas kernels, mlp(): pl.pallas_call(mlp_kernel, out_shape=[jax.ShapeDtypeStruct(shape, BF16)]...  5.68 us
  transfers between devices with their start and end apart: 33, of which 30 were waited for; matrix products, arithmetic and copies ran while one was open for 4% of the time, Pallas kernels for 0%

profile of v1, /device:TPU:2, one launch (start us, length us, event | category | flops | bytes accessed | tf_op | source)
XLA Modules:
  0.0 232.6 jit_solution(4759012056058142879)
XLA Ops:
  0.6 7.3 %collective-permute-start = (bf16[48,1152]{1,0:T(8,128)(2,1)}, bf16[48,1152]{1,0:T(8,128)(2,1)S(1)}, u32[]{:S(2)}, u32[]{:S(2)}) collective-permute-start(bf16[48,1152]{1,0:T(8,128)(2,1)} %bitcast.24), channel_id=1, source_target_pairs={{0,1},{1,0},{2,3},{3,2},{4,5},{5,4},{6,7},{7,6},{8,9},{9,8},{10,11... | collective-permute-start | bytes 331784 | tf_op jit(solution)/shard_map/ppermute | solution.py:54
  12.3 1.6 collective-permute-start.3
  15.0 2.3 collective-permute-start.1
  20.8 3.0 %collective-permute-done.2.x2 = bf16[96,1152]{1,0:T(8,128)(2,1)S(1)} collective-permute-done((bf16[96,1152]{1,0:T(8,128)(2,1)S(1)}, bf16[96,1152]{1,0:T(8,128)(2,1)S(1)}, u32[]{:S(2)}, u32[]{:S(2)}) %collective-permute-start.2) | collective-permute-done | bytes 221216 | tf_op jit(solution)/shard_map/ppermute | solution.py:58
  23.8 2.0 collective-permute-done.1.x1
  25.7 19.9 %attention.2 = (bf16[2,144,384]{2,1,0:T(8,128)(2,1)S(1)}, bf16[96,1152]{1,0:T(8,128)(2,1)S(1)}, bf16[96,1152]{1,0:T(8,128)(2,1)S(1)}, bf16[96,1152]{1,0:T(8,128)(2,1)S(1)}, bf16[96,1152]{1,0:T(8,128)(2,1)S(1)}) custom-call(s32[2]{0:T(128)S(1)} %pad_add_fusion.patch_ref, bf16[96,1152]{1,0:T(8,128)(2,1)S(1)} %maximum_select_fusion.x0.x_ref, ...), custom_call_target="tpu_custom_call" | custom-call | flops 4000000000 | bytes 8000000 | tf_op jit(solution)/shard_map/attention/pallas_call | solution.py:140
  50.7 4.1 %collective-permute-done.4 = bf16[96,1152]{1,0:T(8,128)(2,1)S(1)} collective-permute-done((bf16[96,1152]{1,0:T(8,128)(2,1)S(1)}, bf16[96,1152]{1,0:T(8,128)(2,1)S(1)}, u32[]{:S(2)}, u32[]{:S(2)}) %collective-permute-start.4) | collective-permute-done | bytes 221216 | tf_op jit(solution)/shard_map/ppermute | solution.py:58
  54.8 2.3 %collective-permute-done.5 = bf16[96,1152]{1,0:T(8,128)(2,1)S(1)} collective-permute-done((bf16[96,1152]{1,0:T(8,128)(2,1)S(1)}, bf16[96,1152]{1,0:T(8,128)(2,1)S(1)}, u32[]{:S(2)}, u32[]{:S(2)}) %collective-permute-start.5) | collective-permute-done | bytes 221216 | tf_op jit(solution)/shard_map/ppermute | solution.py:58
  57.1 1.9 collective-permute-done.6
  59.1 3.8 %collective-permute-start.7 = (bf16[96,1152]{1,0:T(8,128)(2,1)S(1)}, bf16[96,1152]{1,0:T(8,128)(2,1)S(1)}, u32[]{:S(2)}, u32[]{:S(2)}) collective-permute-start(bf16[96,1152]{1,0:T(8,128)(2,1)S(1)} %add_convert_fusion.3.own), channel_id=1, source_target_pairs={{0,1},{1,0},{2,3},{3,2},{4,5},{5,4},{6,7},{7,6},{8,9},{9,8},{10,11... | collective-permute-start | bytes 663560 | tf_op jit(solution)/shard_map/ppermute | solution.py:54
  62.9 6.9 %collective-permute-done.7.other = bf16[96,1152]{1,0:T(8,128)(2,1)S(1)} collective-permute-done((bf16[96,1152]{1,0:T(8,128)(2,1)S(1)}, bf16[96,1152]{1,0:T(8,128)(2,1)S(1)}, u32[]{:S(2)}, u32[]{:S(2)}) %collective-permute-start.7) | collective-permute-done | bytes 221216 | tf_op jit(solution)/shard_map/ppermute | solution.py:54
  70.5 2.1 mlp_input.2
  72.9 1.9 collective-permute-start.10
  77.3 2.1 copy.13
  80.8 1.8 collective-permute-done.10.x2
  82.5 1.9 collective-permute-done.9.x1
  84.5 3.0 %mlp.2 = (bf16[96,1152]{1,0:T(8,128)(2,1)S(1)}, bf16[96,1152]{1,0:T(8,128)(2,1)S(1)}, bf16[96,1152]{1,0:T(8,128)(2,1)S(1)}, bf16[96,1152]{1,0:T(8,128)(2,1)S(1)}) custom-call(bf16[96,1152]{1,0:T(8,128)(2,1)S(1)} %copy-done.8, bf16[96,1152]{1,0:T(8,128)(2,1)} %collective-permute-done.9.x1, bf16[96,1152]{1,0:T(8,128)(2,1)} %collective-permute-done.10.x2, ...), custom_call_target="tpu_custom_call" | custom-call | flops 1000000000 | bytes 5000000 | tf_op jit(solution)/shard_map/mlp/pallas_call | solution.py:194
  87.7 11.9 %collective-permute-start.15 = (bf16[96,1152]{1,0:T(8,128)(2,1)S(1)}, bf16[96,1152]{1,0:T(8,128)(2,1)S(1)}, u32[]{:S(2)}, u32[]{:S(2)}) collective-permute-start(bf16[96,1152]{1,0:T(8,128)(2,1)S(1)} %get-tuple-element.33), channel_id=1, source_target_pairs={{0,14},{1,15},{2,8},{3,9},{4,10},{5,11},{6,12},{7,13},{8,22},{9,23... | collective-permute-start | bytes 663560 | tf_op jit(solution)/shard_map/ppermute | solution.py:62
  99.6 3.4 %collective-permute-done.12 = bf16[96,1152]{1,0:T(8,128)(2,1)S(1)} collective-permute-done((bf16[96,1152]{1,0:T(8,128)(2,1)S(1)}, bf16[96,1152]{1,0:T(8,128)(2,1)S(1)}, u32[]{:S(2)}, u32[]{:S(2)}) %collective-permute-start.12) | collective-permute-done | bytes 221216 | tf_op jit(solution)/shard_map/ppermute | solution.py:62
  103.1 3.3 %collective-permute-done.14 = bf16[96,1152]{1,0:T(8,128)(2,1)S(1)} collective-permute-done((bf16[96,1152]{1,0:T(8,128)(2,1)S(1)}, bf16[96,1152]{1,0:T(8,128)(2,1)S(1)}, u32[]{:S(2)}, u32[]{:S(2)}) %collective-permute-start.14) | collective-permute-done | bytes 221216 | tf_op jit(solution)/shard_map/ppermute | solution.py:62
  108.1 5.7 %collective-permute-start.16 = (bf16[96,1152]{1,0:T(8,128)(2,1)S(1)}, bf16[96,1152]{1,0:T(8,128)(2,1)S(1)}, u32[]{:S(2)}, u32[]{:S(2)}) collective-permute-start(bf16[96,1152]{1,0:T(8,128)(2,1)S(1)} %add_convert_fusion.2), channel_id=1, source_target_pairs={{0,1},{1,0},{2,3},{3,2},{4,5},{5,4},{6,7},{7,6},{8,9},{9,8},{10,11... | collective-permute-start | bytes 663560 | tf_op jit(solution)/shard_map/ppermute | solution.py:54
  114.7 5.6 %collective-permute-done.16 = bf16[96,1152]{1,0:T(8,128)(2,1)S(1)} collective-permute-done((bf16[96,1152]{1,0:T(8,128)(2,1)S(1)}, bf16[96,1152]{1,0:T(8,128)(2,1)S(1)}, u32[]{:S(2)}, u32[]{:S(2)}) %collective-permute-start.16) | collective-permute-done | bytes 221216 | tf_op jit(solution)/shard_map/ppermute | solution.py:54
  120.3 2.0 collective-permute-start.19
  122.3 5.7 %collective-permute-start.18 = (bf16[96,1152]{1,0:T(8,128)(2,1)S(1)}, bf16[96,1152]{1,0:T(8,128)(2,1)S(1)}, u32[]{:S(2)}, u32[]{:S(2)}) collective-permute-start(bf16[96,1152]{1,0:T(8,128)(2,1)S(1)} %add_convert_fusion.1.x0.x_ref), channel_id=1, source_target_pairs={{0,4},{1,5},{2,6},{3,7},{4,0},{5,1},{6,2},{7,3},{8,12},{9,13},{10,... | collective-permute-start | bytes 663560 | tf_op jit(solution)/shard_map/ppermute | solution.py:58
  127.9 2.5 %collective-permute-start.17 = (bf16[96,1152]{1,0:T(8,128)(2,1)S(1)}, bf16[96,1152]{1,0:T(8,128)(2,1)S(1)}, u32[]{:S(2)}, u32[]{:S(2)}) collective-permute-start(bf16[96,1152]{1,0:T(8,128)(2,1)S(1)} %add_convert_fusion.1.x0.x_ref), channel_id=1, source_target_pairs={{0,6},{1,7},{2,0},{3,1},{4,2},{5,3},{6,4},{7,5},{8,14},{9,15},{10,... | collective-permute-start | bytes 663560 | tf_op jit(solution)/shard_map/ppermute | solution.py:58
  130.5 3.8 %collective-permute-done.18.x2 = bf16[96,1152]{1,0:T(8,128)(2,1)S(1)} collective-permute-done((bf16[96,1152]{1,0:T(8,128)(2,1)S(1)}, bf16[96,1152]{1,0:T(8,128)(2,1)S(1)}, u32[]{:S(2)}, u32[]{:S(2)}) %collective-permute-start.18) | collective-permute-done | bytes 221216 | tf_op jit(solution)/shard_map/ppermute | solution.py:58
  134.3 2.9 %collective-permute-done.17.x1 = bf16[96,1152]{1,0:T(8,128)(2,1)S(1)} collective-permute-done((bf16[96,1152]{1,0:T(8,128)(2,1)S(1)}, bf16[96,1152]{1,0:T(8,128)(2,1)S(1)}, u32[]{:S(2)}, u32[]{:S(2)}) %collective-permute-start.17) | collective-permute-done | bytes 221216 | tf_op jit(solution)/shard_map/ppermute | solution.py:58
  137.2 19.9 %attention.3 = (bf16[2,144,384]{2,1,0:T(8,128)(2,1)S(1)}, bf16[96,1152]{1,0:T(8,128)(2,1)S(1)}, bf16[96,1152]{1,0:T(8,128)(2,1)S(1)}, bf16[96,1152]{1,0:T(8,128)(2,1)S(1)}, bf16[96,1152]{1,0:T(8,128)(2,1)S(1)}) custom-call(s32[2]{0:T(128)S(1)} %pad_add_fusion.patch_ref, bf16[96,1152]{1,0:T(8,128)(2,1)S(1)} %add_convert_fusion.1.x0.x_ref, ...), custom_call_target="tpu_custom_call" | custom-call | flops 4000000000 | bytes 8000000 | tf_op jit(solution)/shard_map/attention/pallas_call | solution.py:140
  157.7 3.8 %collective-permute-start.21 = (bf16[96,1152]{1,0:T(8,128)(2,1)S(1)}, bf16[96,1152]{1,0:T(8,128)(2,1)S(1)}, u32[]{:S(2)}, u32[]{:S(2)}) collective-permute-start(bf16[96,1152]{1,0:T(8,128)(2,1)S(1)} %get-tuple-element.37), channel_id=1, source_target_pairs={{0,4},{1,5},{2,6},{3,7},{4,0},{5,1},{6,2},{7,3},{8,12},{9,13},{10,... | collective-permute-start | bytes 663560 | tf_op jit(solution)/shard_map/ppermute | solution.py:58
  161.5 1.6 collective-permute-start.22
  163.1 1.9 collective-permute-done.20
  165.0 2.8 %collective-permute-done.21 = bf16[96,1152]{1,0:T(8,128)(2,1)S(1)} collective-permute-done((bf16[96,1152]{1,0:T(8,128)(2,1)S(1)}, bf16[96,1152]{1,0:T(8,128)(2,1)S(1)}, u32[]{:S(2)}, u32[]{:S(2)}) %collective-permute-start.21) | collective-permute-done | bytes 221216 | tf_op jit(solution)/shard_map/ppermute | solution.py:58
  167.8 2.9 %collective-permute-done.22 = bf16[96,1152]{1,0:T(8,128)(2,1)S(1)} collective-permute-done((bf16[96,1152]{1,0:T(8,128)(2,1)S(1)}, bf16[96,1152]{1,0:T(8,128)(2,1)S(1)}, u32[]{:S(2)}, u32[]{:S(2)}) %collective-permute-start.22) | collective-permute-done | bytes 221216 | tf_op jit(solution)/shard_map/ppermute | solution.py:58
  171.0 15.7 %collective-permute-done.23.other = bf16[96,1152]{1,0:T(8,128)(2,1)} collective-permute-done((bf16[96,1152]{1,0:T(8,128)(2,1)S(1)}, bf16[96,1152]{1,0:T(8,128)(2,1)}, u32[]{:S(2)}, u32[]{:S(2)}) %collective-permute-start.23) | collective-permute-done | bytes 221216 | tf_op jit(solution)/shard_map/ppermute | solution.py:54
  186.7 2.1 mlp_input.3
  188.8 3.7 %collective-permute-start.26 = (bf16[96,1152]{1,0:T(8,128)(2,1)}, bf16[96,1152]{1,0:T(8,128)(2,1)S(1)}, u32[]{:S(2)}, u32[]{:S(2)}) collective-permute-start(bf16[96,1152]{1,0:T(8,128)(2,1)} %get-tuple-element.40.x0), channel_id=1, source_target_pairs={{0,4},{1,5},{2,6},{3,7},{4,0},{5,1},{6,2},{7,3},{8,12},{9,13},{10,... | collective-permute-start | bytes 663560 | tf_op jit(solution)/shard_map/ppermute | solution.py:58
  192.5 2.6 %collective-permute-start.25 = (bf16[96,1152]{1,0:T(8,128)(2,1)}, bf16[96,1152]{1,0:T(8,128)(2,1)S(1)}, u32[]{:S(2)}, u32[]{:S(2)}) collective-permute-start(bf16[96,1152]{1,0:T(8,128)(2,1)} %get-tuple-element.40.x0), channel_id=1, source_target_pairs={{0,6},{1,7},{2,0},{3,1},{4,2},{5,3},{6,4},{7,5},{8,14},{9,15},{10,... | collective-permute-start | bytes 663560 | tf_op jit(solution)/shard_map/ppermute | solution.py:58
  195.1 1.6 collective-permute-done.26.x2
  196.7 2.3 %collective-permute-done.25.x1 = bf16[96,1152]{1,0:T(8,128)(2,1)S(1)} collective-permute-done((bf16[96,1152]{1,0:T(8,128)(2,1)}, bf16[96,1152]{1,0:T(8,128)(2,1)S(1)}, u32[]{:S(2)}, u32[]{:S(2)}) %collective-permute-start.25) | collective-permute-done | bytes 221216 | tf_op jit(solution)/shard_map/ppermute | solution.py:58
  200.0 2.7 %mlp.3 = (bf16[96,1152]{1,0:T(8,128)(2,1)}, bf16[96,1152]{1,0:T(8,128)(2,1)}, bf16[96,1152]{1,0:T(8,128)(2,1)}, bf16[96,1152]{1,0:T(8,128)(2,1)}) custom-call(bf16[96,1152]{1,0:T(8,128)(2,1)S(1)} %copy-done.7, bf16[96,1152]{1,0:T(8,128)(2,1)S(1)} %collective-permute-done.25.x1, bf16[96,1152]{1,0:T(8,128)(2,1)S(1)} %collective-permute-done.26.x2, ...), custom_call_target="tpu_custom_call" | custom-call | flops 1000000000 | bytes 5000000 | tf_op jit(solution)/shard_map/mlp/pallas_call | solution.py:194
  202.7 2.5 %collective-permute-start.29 = (bf16[96,1152]{1,0:T(8,128)(2,1)}, bf16[96,1152]{1,0:T(8,128)(2,1)S(1)}, u32[]{:S(2)}, u32[]{:S(2)}) collective-permute-start(bf16[96,1152]{1,0:T(8,128)(2,1)} %get-tuple-element.42), channel_id=1, source_target_pairs={{0,10},{1,11},{2,12},{3,13},{4,14},{5,15},{6,8},{7,9},{8,18},{9,19... | collective-permute-start | bytes 663560 | tf_op jit(solution)/shard_map/ppermute | solution.py:62
  205.2 1.9 collective-permute-start.30
  207.2 6.8 %collective-permute-start.31 = (bf16[96,1152]{1,0:T(8,128)(2,1)}, bf16[96,1152]{1,0:T(8,128)(2,1)S(1)}, u32[]{:S(2)}, u32[]{:S(2)}) collective-permute-start(bf16[96,1152]{1,0:T(8,128)(2,1)} %get-tuple-element.44), channel_id=1, source_target_pairs={{0,14},{1,15},{2,8},{3,9},{4,10},{5,11},{6,12},{7,13},{8,22},{9,23... | collective-permute-start | bytes 663560 | tf_op jit(solution)/shard_map/ppermute | solution.py:62
  213.9 2.1 collective-permute-done.29
  216.0 4.4 %collective-permute-done.30 = bf16[96,1152]{1,0:T(8,128)(2,1)S(1)} collective-permute-done((bf16[96,1152]{1,0:T(8,128)(2,1)}, bf16[96,1152]{1,0:T(8,128)(2,1)S(1)}, u32[]{:S(2)}, u32[]{:S(2)}) %collective-permute-start.30) | collective-permute-done | bytes 221216 | tf_op jit(solution)/shard_map/ppermute | solution.py:62
  220.5 2.1 collective-permute-done.31
  224.0 2.5 %collective-permute-done.24 = f32[96,1152]{1,0:T(8,128)S(1)} collective-permute-done((f32[96,1152]{1,0:T(8,128)}, f32[96,1152]{1,0:T(8,128)S(1)}, u32[]{:S(2)}, u32[]{:S(2)}) %collective-permute-start.24) | collective-permute-done | bytes 442400 | tf_op jit(solution)/shard_map/ppermute | solution.py:62
  226.5 5.2 %collective-permute-done.32 = bf16[48,1152]{1,0:T(8,128)(2,1)S(1)} collective-permute-done((bf16[48,1152]{1,0:T(8,128)(2,1)S(1)}, bf16[48,1152]{1,0:T(8,128)(2,1)S(1)}, u32[]{:S(2)}, u32[]{:S(2)}) %collective-permute-start.32) | collective-permute-done | bytes 110624 | tf_op jit(solution)/shard_map/ppermute | solution.py:54
  (68 shorter events, 25.0 us)
Async XLA Ops:
  0.6 10.6 %collective-permute-start = (bf16[48,1152]{1,0:T(8,128)(2,1)}, bf16[48,1152]{1,0:T(8,128)(2,1)S(1)}, u32[]{:S(2)}, u32[]{:S(2)}) collective-permute-start(bf16[48,1152]{1,0:T(8,128)(2,1)} %bitcast.24), channel_id=1, source_target_pairs={{0,1},{1,0},{2,3},{3,2},{4,5},{5,4},{6,7},{7,6},{8,9},{9,8},{10,11... | collective-permute-start | bytes 331784 | tf_op jit(solution)/shard_map/ppermute | solution.py:54
  10.6 35.1 %copy-start = (f32[6,1152]{1,0:T(8,128)}, f32[6,1152]{1,0:T(8,128)S(1)}, u32[]{:S(2)}) copy-start(f32[6,1152]{1,0:T(8,128)S(1)} %bitcast_add_fusion.mod) | copy-start | bytes 82948
  12.3 33.4 %copy-start.3 = (bf16[96,1152]{1,0:T(8,128)(2,1)}, bf16[96,1152]{1,0:T(8,128)(2,1)S(1)}, u32[]{:S(2)}) copy-start(bf16[96,1152]{1,0:T(8,128)(2,1)S(1)} %maximum_select_fusion.x0.x_ref) | copy-start | bytes 663556
  12.3 8.4 %collective-permute-start.3 = (bf16[96,1152]{1,0:T(8,128)(2,1)S(1)}, bf16[96,1152]{1,0:T(8,128)(2,1)S(1)}, u32[]{:S(2)}, u32[]{:S(2)}) collective-permute-start(bf16[96,1152]{1,0:T(8,128)(2,1)S(1)} %maximum_select_fusion.x0.x_ref), channel_id=1, source_target_pairs={{0,2},{1,3},{2,4},{3,5},{4,6},{5,7},{6,0},{7,1},{8,10},{9,11},{10,... | collective-permute-start | bytes 663560 | tf_op jit(solution)/shard_map/ppermute | solution.py:58
  13.9 9.9 %collective-permute-start.2 = (bf16[96,1152]{1,0:T(8,128)(2,1)S(1)}, bf16[96,1152]{1,0:T(8,128)(2,1)S(1)}, u32[]{:S(2)}, u32[]{:S(2)}) collective-permute-start(bf16[96,1152]{1,0:T(8,128)(2,1)S(1)} %maximum_select_fusion.x0.x_ref), channel_id=1, source_target_pairs={{0,4},{1,5},{2,6},{3,7},{4,0},{5,1},{6,2},{7,3},{8,12},{9,13},{10,... | collective-permute-start | bytes 663560 | tf_op jit(solution)/shard_map/ppermute | solution.py:58
  15.0 10.7 %collective-permute-start.1 = (bf16[96,1152]{1,0:T(8,128)(2,1)S(1)}, bf16[96,1152]{1,0:T(8,128)(2,1)S(1)}, u32[]{:S(2)}, u32[]{:S(2)}) collective-permute-start(bf16[96,1152]{1,0:T(8,128)(2,1)S(1)} %maximum_select_fusion.x0.x_ref), channel_id=1, source_target_pairs={{0,6},{1,7},{2,0},{3,1},{4,2},{5,3},{6,4},{7,5},{8,14},{9,15},{10,... | collective-permute-start | bytes 663560 | tf_op jit(solution)/shard_map/ppermute | solution.py:58
  45.7 0.7 copy-start.5
  46.4 29.8 %copy-start.9 = (bf16[1,1152,576]{1,2,0:T(8,128)(2,1)S(1)}, bf16[1,1152,576]{1,2,0:T(8,128)(2,1)}, u32[]{:S(2)}) copy-start(bf16[1,1152,576]{1,2,0:T(8,128)(2,1)} %param.14) | copy-start | bytes 3981316
  46.4 8.4 %collective-permute-start.4 = (bf16[96,1152]{1,0:T(8,128)(2,1)S(1)}, bf16[96,1152]{1,0:T(8,128)(2,1)S(1)}, u32[]{:S(2)}, u32[]{:S(2)}) collective-permute-start(bf16[96,1152]{1,0:T(8,128)(2,1)S(1)} %get-tuple-element.25), channel_id=1, source_target_pairs={{0,2},{1,3},{2,4},{3,5},{4,6},{5,7},{6,0},{7,1},{8,10},{9,11},{10,... | collective-permute-start | bytes 663560 | tf_op jit(solution)/shard_map/ppermute | solution.py:58
  47.6 9.5 %collective-permute-start.5 = (bf16[96,1152]{1,0:T(8,128)(2,1)S(1)}, bf16[96,1152]{1,0:T(8,128)(2,1)S(1)}, u32[]{:S(2)}, u32[]{:S(2)}) collective-permute-start(bf16[96,1152]{1,0:T(8,128)(2,1)S(1)} %get-tuple-element.26), channel_id=1, source_target_pairs={{0,4},{1,5},{2,6},{3,7},{4,0},{5,1},{6,2},{7,3},{8,12},{9,13},{10,... | collective-permute-start | bytes 663560 | tf_op jit(solution)/shard_map/ppermute | solution.py:58
  49.1 9.9 %collective-permute-start.6 = (bf16[96,1152]{1,0:T(8,128)(2,1)S(1)}, bf16[96,1152]{1,0:T(8,128)(2,1)S(1)}, u32[]{:S(2)}, u32[]{:S(2)}) collective-permute-start(bf16[96,1152]{1,0:T(8,128)(2,1)S(1)} %get-tuple-element.27), channel_id=1, source_target_pairs={{0,6},{1,7},{2,0},{3,1},{4,2},{5,3},{6,4},{7,5},{8,14},{9,15},{10,... | collective-permute-start | bytes 663560 | tf_op jit(solution)/shard_map/ppermute | solution.py:58
  59.1 10.7 %copy-start.10 = (bf16[96,1152]{1,0:T(8,128)(2,1)}, bf16[96,1152]{1,0:T(8,128)(2,1)S(1)}, u32[]{:S(2)}) copy-start(bf16[96,1152]{1,0:T(8,128)(2,1)S(1)} %add_convert_fusion.3.own) | copy-start | bytes 663556
  59.1 10.7 %collective-permute-start.7 = (bf16[96,1152]{1,0:T(8,128)(2,1)S(1)}, bf16[96,1152]{1,0:T(8,128)(2,1)S(1)}, u32[]{:S(2)}, u32[]{:S(2)}) collective-permute-start(bf16[96,1152]{1,0:T(8,128)(2,1)S(1)} %add_convert_fusion.3.own), channel_id=1, source_target_pairs={{0,1},{1,0},{2,3},{3,2},{4,5},{5,4},{6,7},{7,6},{8,9},{9,8},{10,11... | collective-permute-start | bytes 663560 | tf_op jit(solution)/shard_map/ppermute | solution.py:54
  69.8 0.7 copy-start.12
  72.6 8.2 %collective-permute-start.11 = (bf16[96,1152]{1,0:T(8,128)(2,1)}, bf16[96,1152]{1,0:T(8,128)(2,1)S(1)}, u32[]{:S(2)}, u32[]{:S(2)}) collective-permute-start(bf16[96,1152]{1,0:T(8,128)(2,1)} %get-tuple-element.29.x0), channel_id=1, source_target_pairs={{0,2},{1,3},{2,4},{3,5},{4,6},{5,7},{6,0},{7,1},{8,10},{9,11},{10,... | collective-permute-start | bytes 663560 | tf_op jit(solution)/shard_map/ppermute | solution.py:58
  72.9 9.6 %collective-permute-start.10 = (bf16[96,1152]{1,0:T(8,128)(2,1)}, bf16[96,1152]{1,0:T(8,128)(2,1)}, u32[]{:S(2)}, u32[]{:S(2)}) collective-permute-start(bf16[96,1152]{1,0:T(8,128)(2,1)} %get-tuple-element.29.x0), channel_id=1, source_target_pairs={{0,4},{1,5},{2,6},{3,7},{4,0},{5,1},{6,2},{7,3},{8,12},{9,13},{10,... | collective-permute-start | bytes 663560 | tf_op jit(solution)/shard_map/ppermute | solution.py:58
  74.8 9.7 %collective-permute-start.9 = (bf16[96,1152]{1,0:T(8,128)(2,1)}, bf16[96,1152]{1,0:T(8,128)(2,1)}, u32[]{:S(2)}, u32[]{:S(2)}) collective-permute-start(bf16[96,1152]{1,0:T(8,128)(2,1)} %get-tuple-element.29.x0), channel_id=1, source_target_pairs={{0,6},{1,7},{2,0},{3,1},{4,2},{5,3},{6,4},{7,5},{8,14},{9,15},{10,... | collective-permute-start | bytes 663560 | tf_op jit(solution)/shard_map/ppermute | solution.py:58
  77.3 7.2 %copy-start.1 = (f32[6,1152]{1,0:T(8,128)S(1)}, f32[6,1152]{1,0:T(8,128)}, u32[]{:S(2)}) copy-start(f32[6,1152]{1,0:T(8,128)} %copy-done) | copy-start | bytes 82948
  77.3 7.1 %copy-start.8 = (bf16[96,1152]{1,0:T(8,128)(2,1)S(1)}, bf16[96,1152]{1,0:T(8,128)(2,1)}, u32[]{:S(2)}) copy-start(bf16[96,1152]{1,0:T(8,128)(2,1)} %get-tuple-element.29.x0) | copy-start | bytes 663556
  84.5 15.1 %copy-start.13 = (f32[96,1152]{1,0:T(8,128)S(1)}, f32[96,1152]{1,0:T(8,128)}, u32[]{:S(2)}) copy-start(f32[96,1152]{1,0:T(8,128)} %get-tuple-element.28) | copy-start | bytes 1327108
  87.5 15.5 %collective-permute-start.12 = (bf16[96,1152]{1,0:T(8,128)(2,1)S(1)}, bf16[96,1152]{1,0:T(8,128)(2,1)S(1)}, u32[]{:S(2)}, u32[]{:S(2)}) collective-permute-start(bf16[96,1152]{1,0:T(8,128)(2,1)S(1)} %get-tuple-element.30), channel_id=1, source_target_pairs={{0,8},{1,9},{2,10},{3,11},{4,12},{5,13},{6,14},{7,15},{8,16},{9,17... | collective-permute-start | bytes 663560 | tf_op jit(solution)/shard_map/ppermute | solution.py:62
  87.5 15.6 %collective-permute-start.13 = (bf16[96,1152]{1,0:T(8,128)(2,1)S(1)}, bf16[96,1152]{1,0:T(8,128)(2,1)S(1)}, u32[]{:S(2)}, u32[]{:S(2)}) collective-permute-start(bf16[96,1152]{1,0:T(8,128)(2,1)S(1)} %get-tuple-element.31), channel_id=1, source_target_pairs={{0,10},{1,11},{2,12},{3,13},{4,14},{5,15},{6,8},{7,9},{8,18},{9,19... | collective-permute-start | bytes 663560 | tf_op jit(solution)/shard_map/ppermute | solution.py:62
  87.6 18.9 %collective-permute-start.14 = (bf16[96,1152]{1,0:T(8,128)(2,1)S(1)}, bf16[96,1152]{1,0:T(8,128)(2,1)S(1)}, u32[]{:S(2)}, u32[]{:S(2)}) collective-permute-start(bf16[96,1152]{1,0:T(8,128)(2,1)S(1)} %get-tuple-element.32), channel_id=1, source_target_pairs={{0,12},{1,13},{2,14},{3,15},{4,8},{5,9},{6,10},{7,11},{8,20},{9,21... | collective-permute-start | bytes 663560 | tf_op jit(solution)/shard_map/ppermute | solution.py:62
  87.7 20.3 %collective-permute-start.15 = (bf16[96,1152]{1,0:T(8,128)(2,1)S(1)}, bf16[96,1152]{1,0:T(8,128)(2,1)S(1)}, u32[]{:S(2)}, u32[]{:S(2)}) collective-permute-start(bf16[96,1152]{1,0:T(8,128)(2,1)S(1)} %get-tuple-element.33), channel_id=1, source_target_pairs={{0,14},{1,15},{2,8},{3,9},{4,10},{5,11},{6,12},{7,13},{8,22},{9,23... | collective-permute-start | bytes 663560 | tf_op jit(solution)/shard_map/ppermute | solution.py:62
  99.6 15.0 %collective-permute-start.8 = (f32[96,1152]{1,0:T(8,128)S(1)}, f32[96,1152]{1,0:T(8,128)S(1)}, u32[]{:S(2)}, u32[]{:S(2)}) collective-permute-start(f32[96,1152]{1,0:T(8,128)S(1)} %copy-done.13), channel_id=1, source_target_pairs={{0,8},{1,9},{2,10},{3,11},{4,12},{5,13},{6,14},{7,15},{8,16},{9,17... | collective-permute-start | bytes 1327112 | tf_op jit(solution)/shard_map/ppermute | solution.py:62
  108.1 12.1 %collective-permute-start.16 = (bf16[96,1152]{1,0:T(8,128)(2,1)S(1)}, bf16[96,1152]{1,0:T(8,128)(2,1)S(1)}, u32[]{:S(2)}, u32[]{:S(2)}) collective-permute-start(bf16[96,1152]{1,0:T(8,128)(2,1)S(1)} %add_convert_fusion.2), channel_id=1, source_target_pairs={{0,1},{1,0},{2,3},{3,2},{4,5},{5,4},{6,7},{7,6},{8,9},{9,8},{10,11... | collective-permute-start | bytes 663560 | tf_op jit(solution)/shard_map/ppermute | solution.py:54
  120.3 36.8 %copy-start.4 = (bf16[96,1152]{1,0:T(8,128)(2,1)}, bf16[96,1152]{1,0:T(8,128)(2,1)S(1)}, u32[]{:S(2)}) copy-start(bf16[96,1152]{1,0:T(8,128)(2,1)S(1)} %add_convert_fusion.1.x0.x_ref) | copy-start | bytes 663556
  120.3 10.2 %collective-permute-start.19 = (bf16[96,1152]{1,0:T(8,128)(2,1)S(1)}, bf16[96,1152]{1,0:T(8,128)(2,1)S(1)}, u32[]{:S(2)}, u32[]{:S(2)}) collective-permute-start(bf16[96,1152]{1,0:T(8,128)(2,1)S(1)} %add_convert_fusion.1.x0.x_ref), channel_id=1, source_target_pairs={{0,2},{1,3},{2,4},{3,5},{4,6},{5,7},{6,0},{7,1},{8,10},{9,11},{10,... | collective-permute-start | bytes 663560 | tf_op jit(solution)/shard_map/ppermute | solution.py:58
  122.3 12.0 %collective-permute-start.18 = (bf16[96,1152]{1,0:T(8,128)(2,1)S(1)}, bf16[96,1152]{1,0:T(8,128)(2,1)S(1)}, u32[]{:S(2)}, u32[]{:S(2)}) collective-permute-start(bf16[96,1152]{1,0:T(8,128)(2,1)S(1)} %add_convert_fusion.1.x0.x_ref), channel_id=1, source_target_pairs={{0,4},{1,5},{2,6},{3,7},{4,0},{5,1},{6,2},{7,3},{8,12},{9,13},{10,... | collective-permute-start | bytes 663560 | tf_op jit(solution)/shard_map/ppermute | solution.py:58
  127.9 9.3 %collective-permute-start.17 = (bf16[96,1152]{1,0:T(8,128)(2,1)S(1)}, bf16[96,1152]{1,0:T(8,128)(2,1)S(1)}, u32[]{:S(2)}, u32[]{:S(2)}) collective-permute-start(bf16[96,1152]{1,0:T(8,128)(2,1)S(1)} %add_convert_fusion.1.x0.x_ref), channel_id=1, source_target_pairs={{0,6},{1,7},{2,0},{3,1},{4,2},{5,3},{6,4},{7,5},{8,14},{9,15},{10,... | collective-permute-start | bytes 663560 | tf_op jit(solution)/shard_map/ppermute | solution.py:58
  157.1 42.0 %copy-start.2 = (f32[6,1152]{1,0:T(8,128)S(1)}, f32[6,1152]{1,0:T(8,128)}, u32[]{:S(2)}) copy-start(f32[6,1152]{1,0:T(8,128)} %copy-done) | copy-start | bytes 82948
  157.1 7.9 %collective-permute-start.20 = (bf16[96,1152]{1,0:T(8,128)(2,1)S(1)}, bf16[96,1152]{1,0:T(8,128)(2,1)S(1)}, u32[]{:S(2)}, u32[]{:S(2)}) collective-permute-start(bf16[96,1152]{1,0:T(8,128)(2,1)S(1)} %get-tuple-element.36), channel_id=1, source_target_pairs={{0,2},{1,3},{2,4},{3,5},{4,6},{5,7},{6,0},{7,1},{8,10},{9,11},{10,... | collective-permute-start | bytes 663560 | tf_op jit(solution)/shard_map/ppermute | solution.py:58
  157.7 10.1 %collective-permute-start.21 = (bf16[96,1152]{1,0:T(8,128)(2,1)S(1)}, bf16[96,1152]{1,0:T(8,128)(2,1)S(1)}, u32[]{:S(2)}, u32[]{:S(2)}) collective-permute-start(bf16[96,1152]{1,0:T(8,128)(2,1)S(1)} %get-tuple-element.37), channel_id=1, source_target_pairs={{0,4},{1,5},{2,6},{3,7},{4,0},{5,1},{6,2},{7,3},{8,12},{9,13},{10,... | collective-permute-start | bytes 663560 | tf_op jit(solution)/shard_map/ppermute | solution.py:58
  161.5 9.2 %collective-permute-start.22 = (bf16[96,1152]{1,0:T(8,128)(2,1)S(1)}, bf16[96,1152]{1,0:T(8,128)(2,1)S(1)}, u32[]{:S(2)}, u32[]{:S(2)}) collective-permute-start(bf16[96,1152]{1,0:T(8,128)(2,1)S(1)} %get-tuple-element.38), channel_id=1, source_target_pairs={{0,6},{1,7},{2,0},{3,1},{4,2},{5,3},{6,4},{7,5},{8,14},{9,15},{10,... | collective-permute-start | bytes 663560 | tf_op jit(solution)/shard_map/ppermute | solution.py:58
  170.8 15.8 %copy-start.11 = (bf16[96,1152]{1,0:T(8,128)(2,1)}, bf16[96,1152]{1,0:T(8,128)(2,1)S(1)}, u32[]{:S(2)}) copy-start(bf16[96,1152]{1,0:T(8,128)(2,1)S(1)} %add_convert_fusion.own) | copy-start | bytes 663556
  170.9 15.8 %collective-permute-start.23 = (bf16[96,1152]{1,0:T(8,128)(2,1)S(1)}, bf16[96,1152]{1,0:T(8,128)(2,1)}, u32[]{:S(2)}, u32[]{:S(2)}) collective-permute-start(bf16[96,1152]{1,0:T(8,128)(2,1)S(1)} %add_convert_fusion.own), channel_id=1, source_target_pairs={{0,1},{1,0},{2,3},{3,2},{4,5},{5,4},{6,7},{7,6},{8,9},{9,8},{10,11... | collective-permute-start | bytes 663560 | tf_op jit(solution)/shard_map/ppermute | solution.py:54
  188.8 6.3 %collective-permute-start.27 = (bf16[96,1152]{1,0:T(8,128)(2,1)}, bf16[96,1152]{1,0:T(8,128)(2,1)S(1)}, u32[]{:S(2)}, u32[]{:S(2)}) collective-permute-start(bf16[96,1152]{1,0:T(8,128)(2,1)} %get-tuple-element.40.x0), channel_id=1, source_target_pairs={{0,2},{1,3},{2,4},{3,5},{4,6},{5,7},{6,0},{7,1},{8,10},{9,11},{10,... | collective-permute-start | bytes 663560 | tf_op jit(solution)/shard_map/ppermute | solution.py:58
  188.8 7.9 %collective-permute-start.26 = (bf16[96,1152]{1,0:T(8,128)(2,1)}, bf16[96,1152]{1,0:T(8,128)(2,1)S(1)}, u32[]{:S(2)}, u32[]{:S(2)}) collective-permute-start(bf16[96,1152]{1,0:T(8,128)(2,1)} %get-tuple-element.40.x0), channel_id=1, source_target_pairs={{0,4},{1,5},{2,6},{3,7},{4,0},{5,1},{6,2},{7,3},{8,12},{9,13},{10,... | collective-permute-start | bytes 663560 | tf_op jit(solution)/shard_map/ppermute | solution.py:58
  192.5 6.5 %collective-permute-start.25 = (bf16[96,1152]{1,0:T(8,128)(2,1)}, bf16[96,1152]{1,0:T(8,128)(2,1)S(1)}, u32[]{:S(2)}, u32[]{:S(2)}) collective-permute-start(bf16[96,1152]{1,0:T(8,128)(2,1)} %get-tuple-element.40.x0), channel_id=1, source_target_pairs={{0,6},{1,7},{2,0},{3,1},{4,2},{5,3},{6,4},{7,5},{8,14},{9,15},{10,... | collective-permute-start | bytes 663560 | tf_op jit(solution)/shard_map/ppermute | solution.py:58
  199.0 0.9 copy-start.7
  202.7 20.2 %copy-start.6 = (bf16[2,144,384]{2,1,0:T(8,128)(2,1)S(1)}, bf16[2,144,384]{2,1,0:T(8,128)(2,1)}, u32[]{:S(2)}) copy-start(bf16[2,144,384]{2,1,0:T(8,128)(2,1)} %copy-done.5) | copy-start | bytes 663556
  202.7 11.2 %collective-permute-start.28 = (bf16[96,1152]{1,0:T(8,128)(2,1)}, bf16[96,1152]{1,0:T(8,128)(2,1)S(1)}, u32[]{:S(2)}, u32[]{:S(2)}) collective-permute-start(bf16[96,1152]{1,0:T(8,128)(2,1)} %get-tuple-element.41), channel_id=1, source_target_pairs={{0,8},{1,9},{2,10},{3,11},{4,12},{5,13},{6,14},{7,15},{8,16},{9,17... | collective-permute-start | bytes 663560 | tf_op jit(solution)/shard_map/ppermute | solution.py:62
  202.7 13.3 %collective-permute-start.29 = (bf16[96,1152]{1,0:T(8,128)(2,1)}, bf16[96,1152]{1,0:T(8,128)(2,1)S(1)}, u32[]{:S(2)}, u32[]{:S(2)}) collective-permute-start(bf16[96,1152]{1,0:T(8,128)(2,1)} %get-tuple-element.42), channel_id=1, source_target_pairs={{0,10},{1,11},{2,12},{3,13},{4,14},{5,15},{6,8},{7,9},{8,18},{9,19... | collective-permute-start | bytes 663560 | tf_op jit(solution)/shard_map/ppermute | solution.py:62
  205.2 15.2 %collective-permute-start.30 = (bf16[96,1152]{1,0:T(8,128)(2,1)}, bf16[96,1152]{1,0:T(8,128)(2,1)S(1)}, u32[]{:S(2)}, u32[]{:S(2)}) collective-permute-start(bf16[96,1152]{1,0:T(8,128)(2,1)} %get-tuple-element.43), channel_id=1, source_target_pairs={{0,12},{1,13},{2,14},{3,15},{4,8},{5,9},{6,10},{7,11},{8,20},{9,21... | collective-permute-start | bytes 663560 | tf_op jit(solution)/shard_map/ppermute | solution.py:62
  207.2 15.5 %collective-permute-start.31 = (bf16[96,1152]{1,0:T(8,128)(2,1)}, bf16[96,1152]{1,0:T(8,128)(2,1)S(1)}, u32[]{:S(2)}, u32[]{:S(2)}) collective-permute-start(bf16[96,1152]{1,0:T(8,128)(2,1)} %get-tuple-element.44), channel_id=1, source_target_pairs={{0,14},{1,15},{2,8},{3,9},{4,10},{5,11},{6,12},{7,13},{8,22},{9,23... | collective-permute-start | bytes 663560 | tf_op jit(solution)/shard_map/ppermute | solution.py:62
  213.9 12.6 %collective-permute-start.24 = (f32[96,1152]{1,0:T(8,128)}, f32[96,1152]{1,0:T(8,128)S(1)}, u32[]{:S(2)}, u32[]{:S(2)}) collective-permute-start(f32[96,1152]{1,0:T(8,128)} %get-tuple-element.39), channel_id=1, source_target_pairs={{0,8},{1,9},{2,10},{3,11},{4,12},{5,13},{6,14},{7,15},{8,16},{9,17... | collective-permute-start | bytes 1327112 | tf_op jit(solution)/shard_map/ppermute | solution.py:62
  222.8 8.9 %collective-permute-start.32 = (bf16[48,1152]{1,0:T(8,128)(2,1)S(1)}, bf16[48,1152]{1,0:T(8,128)(2,1)S(1)}, u32[]{:S(2)}, u32[]{:S(2)}) collective-permute-start(bf16[48,1152]{1,0:T(8,128)(2,1)S(1)} %select_convert_fusion), channel_id=1, source_target_pairs={{0,1},{1,0},{2,3},{3,2},{4,5},{5,4},{6,7},{7,6},{8,9},{9,8},{10,11... | collective-permute-start | bytes 331784 | tf_op jit(solution)/shard_map/ppermute | solution.py:54
